TPU v7x, 32 devices: a whole 2x2x4 slice. The times are simulated.
32 devices in a mesh: row: 4 (over y, x), col: 8 (over z, core).
Axes of the slice: x: 2, y: 2, z: 4, core: 2. Of those that a mesh axis runs over, the one named last changes fastest.
Arguments:
- tokens: bfloat16 [64, 12288], P('col', 'row'), may hold values from -6 to 6
- cotangent: bfloat16 [64, 12288], P('col', 'row'), may hold values from -3 to 3
- weight_in: bfloat16 [12288, 24576], P('row', 'col'), may hold values from -0.0546875 to 0.0546875
- weight_out: bfloat16 [24576, 12288], P('col', 'row'), may hold values from -0.0390625 to 0.0390625
Outputs:
- mixed: bfloat16 [64, 12288], P('col', 'row')
- grad_tokens: bfloat16 [64, 12288], P('col', 'row')
- grad_in: bfloat16 [12288, 24576], P('row', 'col')
- grad_out: bfloat16 [24576, 12288], P('col', 'row')
All inputs are finite; a program needn't handle non-finite values.
Results may differ from a plain program's by a relative error of at most 0.0049.
Values may be sent and summed in bfloat16 or wider, within the bound.
No kernel may reach another device: no remote copies, remote signals or barrier semaphores. Data moves between devices by JAX's collectives and lax.ppermute only.
A program may use at most 128 MiB of HBM per device.

v0:
```python
import jax
import jax.numpy as jnp
from jax import lax
from jax.sharding import PartitionSpec as P


def gelu_parts(pre_act):
    normal_cdf = 0.5 * (1.0 + jax.scipy.special.erf(pre_act * 0.7071067811865476))
    density = jnp.exp(-0.5 * pre_act * pre_act) * 0.3989422804014327
    return (pre_act * normal_cdf, normal_cdf + pre_act * density)


def contract_first(left_side, right_side):
    return lax.dot_general(
        left_side, right_side, (((0,), (0,)), ((), ())), preferred_element_type=jnp.float32
    )


def contract_last(left_side, right_side):
    return lax.dot_general(
        left_side, right_side, (((1,), (1,)), ((), ())), preferred_element_type=jnp.float32
    )


def width_sums(term_fn, row_count):
    return lax.psum_scatter(
        term_fn(jnp.int32(0), lax.axis_size("row") * row_count),
        "row",
        scatter_dimension=0,
        tiled=True,
    )


def token_spread(row_piece):
    return lax.all_gather(row_piece, "row", axis=0, tiled=True)


def unit_sums(term_fn, row_count):
    return lax.psum_scatter(
        term_fn(jnp.int32(0), lax.axis_size("col") * row_count),
        "col",
        scatter_dimension=0,
        tiled=True,
    )


def shards(tokens, cotangent, weight_in, weight_out):
    tok_all, cot_all = (
        lax.all_gather(tokens, "col", axis=0, tiled=True),
        lax.all_gather(cotangent, "col", axis=0, tiled=True),
    )
    total_rows = tok_all.shape[0]
    share_rows = total_rows // lax.axis_size("row")
    col_rows = total_rows // lax.axis_size("col")

    def forward_term(first_row, row_count):
        return jnp.dot(tok_all, weight_in, preferred_element_type=jnp.float32)

    def backward_term(first_row, row_count):
        return contract_last(cot_all, weight_out)

    pre_share = width_sums(forward_term, share_rows)
    gelu_value, gelu_slope = gelu_parts(pre_share)
    hidden = token_spread(gelu_value.astype(jnp.bfloat16))
    grad_share = width_sums(backward_term, share_rows)
    grad_pre = token_spread((grad_share * gelu_slope).astype(jnp.bfloat16))

    def mix_term(first_row, row_count):
        return jnp.dot(hidden, weight_out, preferred_element_type=jnp.float32)

    def input_term(first_row, row_count):
        return contract_last(grad_pre, weight_in)

    mixed = unit_sums(mix_term, col_rows).astype(jnp.bfloat16)
    grad_in = contract_first(tok_all, grad_pre).astype(jnp.bfloat16)
    grad_out = contract_first(hidden, cot_all).astype(jnp.bfloat16)
    grad_tokens = unit_sums(input_term, col_rows).astype(jnp.bfloat16)
    return (mixed, grad_tokens, grad_in, grad_out)


def solution(mesh):
    return jax.shard_map(
        shards,
        mesh=mesh,
        in_specs=(P("col", "row"), P("col", "row"), P("row", "col"), P("col", "row")),
        out_specs=(P("col", "row"), P("col", "row"), P("row", "col"), P("col", "row")),
        check_vma=False,
    )
```

profile of v0, /device:TPU:0, one launch (start us, length us, event | category | flops | bytes accessed | tf_op | source)
XLA Modules:
  0.0 190.6 jit_solution(15614180086248022942)
XLA Ops:
  7.2 0.0 copy-start
  7.2 0.0 reduce-scatter.9.cloned.1.call-start
  7.2 16.4 %all_gather.14 = bf16[64,3072]{1,0:T(8,128)(2,1)S(1)} all-gather(bf16[8,3072]{1,0:T(8,128)(2,1)} %param.5), channel_id=1, replica_groups=mesh['row'=4,'col'=8] {'col'}, dimensions={0}, use_global_device_ids=true | all-gather | bytes 442368 | tf_op jit(solution)/shard_map/all_gather | solution.py:50
  23.6 13.1 %fusion.8 = f32[64,3072]{1,0:T(8,128)} fusion(bf16[64,3072]{1,0:T(8,128)(2,1)S(1)} %all_gather.14, bf16[3072,3072]{1,0:T(8,128)(2,1)} %param.7), kind=kOutput, calls=%fused_computation.13 | convolution fusion | flops 1207959552 | bytes 20054016 | tf_op jit(solution)/shard_map/dot_general | solution.py:20
  36.7 0.0 reduce-scatter.9.cloned.1.call-update
  36.7 0.0 reduce-scatter.5.cloned.1.call-start
  36.8 0.0 copy-done
  36.8 14.4 %all_gather.12 = bf16[64,3072]{1,0:T(8,128)(2,1)S(1)} all-gather(bf16[8,3072]{1,0:T(8,128)(2,1)S(1)} %copy-done), channel_id=1, replica_groups=mesh['row'=4,'col'=8] {'col'}, dimensions={0}, use_global_device_ids=true | all-gather | bytes 442368 | tf_op jit(solution)/shard_map/all_gather | solution.py:49
  51.2 10.7 %fusion.6 = f32[64,3072]{1,0:T(8,128)} fusion(bf16[64,3072]{1,0:T(8,128)(2,1)S(1)} %all_gather.12, bf16[3072,3072]{1,0:T(8,128)(2,1)} %param.6), kind=kOutput, calls=%fused_computation.11 | convolution fusion | flops 1207959552 | bytes 20054016 | tf_op jit(solution)/shard_map/dot_general | solution.py:57
  61.9 0.0 reduce-scatter.5.cloned.1.call-update
  61.9 0.0 reduce-scatter.7.cloned.1.call-start
  62.0 2.1 %reduce-scatter.9.cloned.1.call-done = f32[16,3072]{1,0:T(8,128)} async-done(((f32[64,3072]{1,0:T(8,128)}), f32[16,3072]{1,0:T(8,128)}) %reduce-scatter.9.cloned.1.call-update) | async-done | bytes 196624 | tf_op jit(solution)/shard_map/reduce_scatter | solution.py:26
  64.1 29.6 %reduce-scatter.5.cloned.1.call-done = f32[16,3072]{1,0:T(8,128)} async-done(((f32[64,3072]{1,0:T(8,128)}), f32[16,3072]{1,0:T(8,128)}) %reduce-scatter.5.cloned.1.call-update) | async-done | bytes 196624 | tf_op jit(solution)/shard_map/reduce_scatter | solution.py:26
  93.7 1.1 fusion.5
  94.8 9.4 %all_gather.13 = bf16[64,3072]{1,0:T(8,128)(2,1)S(1)} all-gather(bf16[16,3072]{1,0:T(8,128)(2,1)S(1)} %get-tuple-element.9), channel_id=1, replica_groups=mesh['row'=4,'col'=8] {'row'}, dimensions={0}, use_global_device_ids=true | all-gather | bytes 491520 | tf_op jit(solution)/shard_map/all_gather | solution.py:35
  104.3 10.6 %fusion.7 = f32[64,3072]{1,0:T(8,128)} fusion(bf16[64,3072]{1,0:T(8,128)(2,1)S(1)} %all_gather.13, bf16[3072,3072]{1,0:T(8,128)(2,1)} %param.7), kind=kOutput, calls=%fused_computation.12 | convolution fusion | flops 1207959552 | bytes 20054016 | tf_op jit(solution)/shard_map/dot_general | solution.py:69
  114.9 0.0 reduce-scatter.7.cloned.1.call-update
  114.9 0.0 reduce-scatter.11.cloned.1.call-start
  115.0 9.3 %all_gather.15 = bf16[64,3072]{1,0:T(8,128)(2,1)S(1)} all-gather(bf16[16,3072]{1,0:T(8,128)(2,1)S(1)} %get-tuple-element.8), channel_id=1, replica_groups=mesh['row'=4,'col'=8] {'row'}, dimensions={0}, use_global_device_ids=true | all-gather | bytes 491520 | tf_op jit(solution)/shard_map/all_gather | solution.py:35
  124.2 13.2 %fusion.9 = f32[64,3072]{1,0:T(8,128)} fusion(bf16[64,3072]{1,0:T(8,128)(2,1)S(1)} %all_gather.15, bf16[3072,3072]{1,0:T(8,128)(2,1)} %param.6), kind=kOutput, calls=%fused_computation.14 | convolution fusion | flops 1207959552 | bytes 20054016 | tf_op jit(solution)/shard_map/dot_general | solution.py:20
  137.4 0.0 reduce-scatter.11.cloned.1.call-update
  137.4 9.5 %convert_bitcast_fusion = bf16[3072,3072]{0,1:T(8,128)(2,1)} fusion(bf16[64,3072]{1,0:T(8,128)(2,1)S(1)} %all_gather.15, bf16[64,3072]{1,0:T(8,128)(2,1)S(1)} %all_gather.12), kind=kOutput, calls=%fused_computation | convolution fusion | flops 1217396736 | bytes 19660800 | tf_op jit(solution)/shard_map/dot_general | solution.py:14
  146.9 24.6 %copy.8 = bf16[3072,3072]{1,0:T(8,128)(2,1)} copy(bf16[3072,3072]{0,1:T(8,128)(2,1)} %convert_bitcast_fusion) | data formatting | bytes 37748736
  171.5 9.5 %convolution_convert_fusion = bf16[3072,3072]{1,0:T(8,128)(2,1)} fusion(bf16[64,3072]{1,0:T(8,128)(2,1)S(1)} %all_gather.13, bf16[64,3072]{1,0:T(8,128)(2,1)S(1)} %all_gather.14), kind=kOutput, calls=%fused_computation.1 | convolution fusion | flops 1217396736 | bytes 19660800 | tf_op jit(solution)/shard_map/dot_general | solution.py:14
  181.0 0.0 reduce-scatter.7.cloned.1.call-done
  181.0 1.5 convert_element_type.22
  182.6 0.0 reduce-scatter.11.cloned.1.call-done
  182.6 1.5 convert_element_type.24
Async XLA Ops:
  7.2 29.6 %copy-start = (bf16[8,3072]{1,0:T(8,128)(2,1)S(1)}, bf16[8,3072]{1,0:T(8,128)(2,1)}, u32[]{:S(2)}) copy-start(bf16[8,3072]{1,0:T(8,128)(2,1)} %param.4) | copy-start | bytes 147460
  7.2 56.9 %reduce-scatter.9.cloned.1.call-start = ((), (), s32[]{:S(2)}) async-start(), calls=%async_computation.6 | async-start | bytes 983040 | tf_op jit(solution)/shard_map/reduce_scatter | solution.py:26
  36.7 57.0 %reduce-scatter.5.cloned.1.call-start = ((), (), s32[]{:S(2)}) async-start(), calls=%async_computation.4 | async-start | bytes 983040 | tf_op jit(solution)/shard_map/reduce_scatter | solution.py:26
  61.9 119.1 %reduce-scatter.7.cloned.1.call-start = ((), (), s32[]{:S(2)}) async-start(), calls=%async_computation.5 | async-start | bytes 884736 | tf_op jit(solution)/shard_map/reduce_scatter | solution.py:39
  114.9 67.6 %reduce-scatter.11.cloned.1.call-start = ((), (), s32[]{:S(2)}) async-start(), calls=%async_computation.7 | async-start | bytes 884736 | tf_op jit(solution)/shard_map/reduce_scatter | solution.py:39
Sparse Core Ops, SparseCore 0:
  36.8 27.2 reduce-scatter.8
  67.6 26.1 reduce-scatter.4
  115.0 31.3 reduce-scatter.6
  148.7 29.8 reduce-scatter.10
where the time goes:
time: 192 us; the launch traced here: 191 us
  matrix products  66.6 us (35%)
  blocking collectives  49.5 us (26%)
  waiting for transfers between devices  31.8 us (17%)
  local copies, waits for them, and re-layouts  24.6 us (13%)
  between operations  13.8 us (7%)
  other arithmetic  4.15 us (2%)
    reduce_scatter x2, waiting for transfers between devices, width_sums(): lax.psum_scatter(term_fn(jnp.int32(0), lax.axis_size('row') * row_count),...  31.7 us
    dot_general x2, matrix products, contract_last(): lax.dot_general(left_side, right_side, (((1,), (1,)), ((), ())), preferre...  26.2 us
    unnamed x3, local copies, waits for them, and re-layouts  24.6 us
    dot_general x2, matrix products, contract_first(): lax.dot_general(left_side, right_side, (((0,), (0,)), ((), ())), preferre...  19 us
    all_gather x2, blocking collectives, token_spread(): return lax.all_gather(row_piece, 'row', axis=0, tiled=True)  18.7 us
    all_gather x1, blocking collectives, shards(): lax.all_gather(cotangent, 'col', axis=0, tiled=True)  16.4 us
    all_gather x1, blocking collectives, shards(): lax.all_gather(tokens, 'col', axis=0, tiled=True)  14.4 us
    dot_general x1, matrix products, forward_term(): return jnp.dot(tok_all, weight_in, preferred_element_type=jnp.float32)  10.7 us
  transfers between devices with their start and end apart: 4, of which 2 were waited for; matrix products, arithmetic and copies ran while one was open for 36% of the time, Pallas kernels for 0%

commit v1 on v0

v1 whole, which is shorter than its diff:
```python
import functools

import jax
import jax.numpy as jnp
from jax import lax
from jax.experimental import pallas as pl
from jax.experimental.pallas import tpu as pltpu
from jax.sharding import PartitionSpec as P

BF = jnp.bfloat16
F32 = jnp.float32
MB = 2**20
CORES = 2
VM = pl.BlockSpec(memory_space=pltpu.VMEM)
ANY = pl.BlockSpec(memory_space=pl.ANY)


def gelu_parts(pre_act):
    normal_cdf = 0.5 * (1.0 + jax.scipy.special.erf(pre_act * 0.7071067811865476))
    density = jnp.exp(-0.5 * pre_act * pre_act) * 0.3989422804014327
    return (pre_act * normal_cdf, normal_cdf + pre_act * density)


def contract_first(left_side, right_side):
    return lax.dot_general(
        left_side, right_side, (((0,), (0,)), ((), ())), preferred_element_type=F32
    )


def contract_last(left_side, right_side):
    return lax.dot_general(
        left_side, right_side, (((1,), (1,)), ((), ())), preferred_element_type=F32
    )


def in_hbm(array):
    return pltpu.with_memory_space_constraint(array, pltpu.HBM)


def chunk_of(size, limit):
    best = 128
    for width in range(128, min(size, limit) + 1, 128):
        if size % width == 0:
            best = width
    return best


def in_vmem(array):
    return pltpu.with_memory_space_constraint(array, pltpu.VMEM)


def call(kernel, args, outs, flops=0, moved=0, limit=6 * MB, scratch=(), aliases=None):
    return pl.pallas_call(
        kernel,
        in_specs=[spec for _, spec in args],
        out_specs=[spec for _, _, spec in outs],
        out_shape=[jax.ShapeDtypeStruct(shape, dtype) for shape, dtype, _ in outs],
        scratch_shapes=list(scratch),
        input_output_aliases=aliases or {},
        compiler_params=pltpu.CompilerParams(vmem_limit_bytes=limit),
        cost_estimate=pl.CostEstimate(flops=flops, bytes_accessed=moved, transcendentals=0),
    )(*[in_hbm(array) if spec is ANY else array for array, spec in args])


def load_kernel(tok, cot, out, tok_v, cot_v, sems):
    copies = [
        pltpu.make_async_copy(tok, tok_v, sems.at[0]),
        pltpu.make_async_copy(cot, cot_v, sems.at[1]),
    ]
    for copy in copies:
        copy.start()
    for copy in copies:
        copy.wait()
    both = [tok_v[...].astype(F32), cot_v[...].astype(F32)]
    out[...] = jnp.concatenate(both, axis=0).astype(BF)


def pack_kernel(after, *refs):
    ins, out = refs[:-1], refs[-1]
    rows = ins[0].shape[0] // 2
    blocks = [ref[...].astype(F32) for ref in ins]
    both = [block[:rows] for block in blocks] + [block[rows:] for block in blocks]
    out[...] = jnp.concatenate(both, axis=0).astype(BF)


def join_rows(mine, other, first, count):
    return jnp.concatenate([mine[first : first + count, :], other[first : first + count, :]], axis=0)


def tok_rows(mine, other):
    half = mine.shape[0] // 2
    return join_rows(mine, other, 0, half)


def cot_rows(mine, other):
    half = mine.shape[0] // 2
    return join_rows(mine, other, half, half)


def block_start(step, block):
    return pl.multiple_of((lax.axis_index("row") ^ step) * block, 128)


def stage_kernel(after, weight, held, sems):
    high = weight.shape[0] // sems.shape[0]
    copies = []
    for j in range(sems.shape[0]):
        at = pl.ds(j * high, high)
        copies.append(pltpu.make_async_copy(weight.at[at, :], held.at[at, :], sems.at[j]))
    for copy in copies:
        copy.start()
    for copy in copies:
        copy.wait()


def forward_kernel(mine, other, weight, *outs):
    block = outs[0].shape[1]
    width = chunk_of(block, 256)
    x = tok_rows(mine, other)
    for step, out in enumerate(outs):
        start = block_start(step, block)

        @pl.loop(0, block // width)
        def _(j):
            at = pl.multiple_of(j * width, 128)
            w = weight[:, pl.ds(pl.multiple_of(start + at, 128), width)]
            part = jnp.dot(x, w, preferred_element_type=F32)
            out[:, pl.ds(at, width)] = part.astype(out.dtype)


def backward_kernel(step, mine, other, pre, weight, out):
    rows, block = pre.shape
    w = weight[pl.ds(block_start(step, block), block), :]
    part = contract_last(w, cot_rows(mine, other)).T.astype(out.dtype)
    if step == 0:
        out[...] = part
    else:
        out[:rows, :] = pre[...]
        out[rows:, :] = part


def gelu_kernel(pre_own, grad_own, *refs):
    parts, out = refs[:-1], refs[-1]
    rows = pre_own.shape[0]
    pre, grad = pre_own[...], grad_own[...]
    for part in parts:
        pre = pre + part[:rows, :].astype(F32)
        grad = grad + part[rows:, :].astype(F32)
    value, slope = gelu_parts(pre)
    out[:rows, :] = value.astype(BF)
    out[rows:, :] = (grad * slope).astype(BF)


def add_up(n, pieces, w_in, w_out, keep, away, hidden, grad, held, sems):
    rows, block = hidden.shape[0], pieces[0].shape[1]
    half = rows // 2
    ring, high = held.shape[0], held.shape[1]
    count = w_in.shape[0] // high

    def copy(j):
        at = pl.ds(pl.multiple_of(j * high, 128), high)
        slot = lax.rem(j, ring)
        return pltpu.make_async_copy(w_in.at[at, :], held.at[slot], sems.at[slot])

    def begin():
        for j in range(ring):
            copy(jnp.int32(j)).start()

    def forward():
        for step, piece in enumerate(pieces):
            columns = pl.ds(block_start(step, block), block)
            hidden[:, columns] = piece[:rows, :]
            grad[:, columns] = piece[rows:, :]
        cols = w_out.shape[1]
        width = chunk_of(cols, 256)

        @pl.loop(0, cols // width)
        def _(j):
            columns = pl.ds(pl.multiple_of(j * width, 128), width)
            part = jnp.dot(hidden[...], w_out[:, columns], preferred_element_type=F32)
            keep[:half, columns] = part[:half]
            away[:half, columns] = part[half:]

    def backward():
        @pl.loop(0, count)
        def _(j):
            copy(j).wait()
            columns = pl.ds(pl.multiple_of(j * high, 128), high)
            part = contract_last(held[lax.rem(j, ring)], grad[...]).T
            keep[half:, columns] = part[:half]
            away[half:, columns] = part[half:]

            @pl.when(j + ring < count)
            def _():
                copy(j + ring).start()

    return begin, forward, backward


def write_grads(step, piece, tok_t, mine, other, grad_in, grad_out, in_v, out_v, in_sems, out_sems):
    rows, block = piece.shape[0] // 2, piece.shape[1]
    start = block_start(step, block)
    cot = cot_rows(mine, other)
    grad = piece[rows:, :]
    n_out, n_in = out_sems.shape[0], in_sems.shape[0]
    chunk, high = out_v.shape[0] // n_out, in_v.shape[0] // n_in

    def out_copy(j):
        at = pl.multiple_of(j * chunk, 128)
        to = pl.multiple_of(start + at, 128)
        return pltpu.make_async_copy(
            out_v.at[pl.ds(at, chunk), :], grad_out.at[pl.ds(to, chunk), :], out_sems.at[j]
        )

    def in_copy(j):
        at = pl.ds(pl.multiple_of(j * high, 128), high)
        return pltpu.make_async_copy(
            in_v.at[at, :], grad_in.at[at, pl.ds(start, block)], in_sems.at[j]
        )

    def product(left, right, place, first):
        tall, wide = chunk_of(left.shape[0], 256), chunk_of(right.shape[1], 256)
        for c in range(right.shape[1] // wide):
            columns = slice(c * wide, (c + 1) * wide)
            for r in range(left.shape[0] // tall):
                part = jnp.dot(
                    left[r * tall : (r + 1) * tall], right[:, columns], preferred_element_type=F32
                )
                at = pl.ds(pl.multiple_of(first + r * tall, 128), tall)
                place[at, columns] = part.astype(BF)

    @pl.loop(0, n_out)
    def _(j):
        first = pl.multiple_of(j * chunk, 128)
        left = piece[:rows, pl.ds(first, chunk)].astype(F32).T.astype(BF)
        product(left, cot, out_v, first)
        out_copy(j).start()

    @pl.loop(0, n_in)
    def _(j):
        first = pl.multiple_of(j * high, 128)
        product(tok_t[pl.ds(first, high), :], grad, in_v, first)
        in_copy(j).start()

    def finish():
        for j in range(n_out):
            out_copy(j).wait()
        for j in range(n_in):
            in_copy(j).wait()

    return finish


def first_kernel(piece, mine, other, _, tok_t, grad_in, grad_out, *scratch):
    tok_t[...] = tok_rows(mine, other).astype(F32).T.astype(BF)
    write_grads(0, piece, tok_t, mine, other, grad_in, grad_out, *[ref.at[0] for ref in scratch])()


def main_kernel(n, steps, *refs):
    pieces = refs[:n]
    mine, other, tok_t, w_in, w_out, _, _, keep, away, grad_in, grad_out = refs[n : n + 11]
    hidden, grad, held, sems = refs[n + 11 : n + 15]
    scratch = refs[n + 15 :]
    begin, forward, backward = add_up(n, pieces, w_in, w_out, keep, away, hidden, grad, held, sems)
    begin()
    for i, step in enumerate(steps):
        own = [ref.at[0] for ref in scratch]
        finish = write_grads(step, pieces[step], tok_t, mine, other, grad_in, grad_out, *own)
        if i == 0:
            forward()
        if i == len(steps) - 1:
            backward()
        finish()


def grads_kernel(steps, *refs):
    pieces = refs[: len(steps)]
    mine, other, tok_t, _, _, grad_in, grad_out = refs[len(steps) : len(steps) + 7]
    scratch = refs[len(steps) + 7 :]
    finish = []
    for i, step in enumerate(steps):
        own = [ref.at[i] for ref in scratch]
        finish.append(write_grads(step, pieces[i], tok_t, mine, other, grad_in, grad_out, *own))
    for end in finish:
        end()


def pair_kernel(keep, away, own, *outs):
    rows = own.shape[0] // 2
    half = keep.shape[0] // 2
    total = keep[...] + away[...]
    for k, out in enumerate((own,) + outs):
        out[:rows, :] = total[k * rows : (k + 1) * rows].astype(out.dtype)
        out[rows:, :] = total[half + k * rows : half + (k + 1) * rows].astype(out.dtype)


def final_kernel(*refs):
    parts, (mixed, back) = refs[:-2], refs[-2:]
    rows = mixed.shape[0]
    total = parts[0][...]
    for part in parts[1:]:
        total = total + part[...].astype(F32)
    mixed[...] = total[:rows].astype(BF)
    back[...] = total[rows:].astype(BF)


def split_plan(tokens, cotangent, weight_in, weight_out):
    n = lax.axis_size("row")
    n_col = lax.axis_size("col")
    z = n_col // CORES
    mine_rows, width = tokens.shape
    units = weight_in.shape[1]
    block = units // n
    rows = mine_rows * n_col
    flops = 2 * rows * width * units

    def along(array, k):
        pairs = []
        for c in range(CORES):
            for at in range(z):
                pairs.append((at * CORES + c, ((at + k) % z) * CORES + c))
        return lax.ppermute(array, "col", pairs)

    def swap(array):
        return lax.ppermute(array, "col", [(i, i ^ 1) for i in range(n_col)])

    def across(array, step):
        return lax.ppermute(array, "row", [(i, i ^ step) for i in range(n)])

    (packed,) = call(
        load_kernel,
        [(tokens, ANY), (cotangent, ANY)],
        [((2 * mine_rows, width), BF, VM)],
        scratch=[pltpu.VMEM((mine_rows, width), BF)] * 2 + [pltpu.SemaphoreType.DMA((2,))],
    )
    others = [along(packed, z - k) for k in range(1, z)]
    (held,) = call(
        stage_kernel,
        [(packed, VM), (weight_in, ANY)],
        [(weight_in.shape, BF, VM)],
        moved=2 * width * units,
        scratch=[pltpu.SemaphoreType.DMA((4,))],
        limit=2 * MB,
    )
    weights = [(in_vmem(held), VM), (in_vmem(weight_out), VM)]
    (mine,) = call(
        pack_kernel,
        [weights[0]] + [(a, VM) for a in [packed] + others],
        [((rows, width), BF, VM)],
    )
    common = [(mine, VM), (swap(mine), VM)]

    pres = call(
        forward_kernel,
        common + weights[:1],
        [((rows, block), F32, VM)] + [((rows, block), BF, VM)] * (n - 1),
        flops=flops,
        moved=2 * width * units,
    )

    def backward(step):
        shape = ((rows, block), F32, VM) if step == 0 else ((2 * rows, block), BF, VM)
        return call(
            functools.partial(backward_kernel, step),
            common + [(pres[step], VM), weights[1]],
            [shape],
            flops=flops // n,
            moved=2 * width * block,
        )[0]

    arrived = [(across(backward(step), step), VM) for step in range(n - 1, 0, -1)]
    own = [pres[0], backward(0)]
    (piece,) = call(
        gelu_kernel, [(a, VM) for a in own] + arrived, [((2 * rows, block), BF, VM)]
    )
    pieces = [piece] + [across(piece, step) for step in range(1, n)]

    grads = [((width, units), BF, ANY), ((units, width), BF, ANY)]
    n_in = width // chunk_of(width, 768)
    n_out = block // chunk_of(block, 256)

    def staging(count):
        return [
            pltpu.VMEM((count, width, block), BF),
            pltpu.VMEM((count, block, width), BF),
            pltpu.SemaphoreType.DMA((count, n_in)),
            pltpu.SemaphoreType.DMA((count, n_out)),
        ]

    tok_t, grad_in, grad_out = call(
        first_kernel,
        [(piece, VM)] + common + [weights[1]],
        [((width, rows), BF, VM)] + grads,
        flops=2 * flops // n,
        moved=4 * width * block,
        scratch=staging(1),
        limit=4 * width * block + 4 * MB,
    )

    inner = list(range(1, n - 1))
    high = chunk_of(width, 768)
    ring = min(2, width // high)
    keep, away, grad_in, grad_out = call(
        functools.partial(main_kernel, n, inner),
        [(a, VM) for a in pieces] + common + [(tok_t, VM), (weight_in, ANY), weights[1]]
        + [(grad_in, ANY), (grad_out, ANY)],
        [((rows, width), F32, VM)] * 2 + grads,
        flops=2 * flops + 2 * len(inner) * flops // n,
        moved=4 * width * units + 4 * len(inner) * width * block,
        scratch=[pltpu.VMEM((rows, units), BF)] * 2
        + [pltpu.VMEM((ring, high, units), BF), pltpu.SemaphoreType.DMA((ring,))]
        + staging(1),
        limit=2 * ring * high * units + 4 * width * block + 5 * MB,
        aliases={n + 5: 2, n + 6: 3},
    )
    away = swap(away)
    totals = call(
        pair_kernel,
        [(keep, VM), (away, VM)],
        [((2 * mine_rows, width), F32, VM)] + [((2 * mine_rows, width), BF, VM)] * (z - 1),
    )
    parts = [totals[0]] + [along(totals[k], k) for k in range(1, z)]
    last = [n - 1]
    grad_in, grad_out = call(
        functools.partial(grads_kernel, last),
        [(pieces[step], VM) for step in last] + common
        + [(tok_t, VM), (grad_in, ANY), (grad_out, ANY)],
        grads,
        flops=2 * flops // n,
        moved=4 * width * block,
        scratch=staging(1),
        limit=4 * width * block + 4 * MB,
        aliases={4: 0, 5: 1},
    )
    mixed, grad_tokens = call(
        final_kernel, [(a, VM) for a in parts], [((mine_rows, width), BF, VM)] * 2
    )
    return (mixed, grad_tokens, grad_in, grad_out)


def plain_plan(tokens, cotangent, weight_in, weight_out):
    tok_all = lax.all_gather(tokens, "col", axis=0, tiled=True)
    cot_all = lax.all_gather(cotangent, "col", axis=0, tiled=True)
    pre = lax.psum_scatter(
        jnp.dot(tok_all, weight_in, preferred_element_type=F32),
        "row", scatter_dimension=0, tiled=True,
    )
    value, slope = gelu_parts(pre)
    hidden = lax.all_gather(value.astype(BF), "row", axis=0, tiled=True)
    grad_hidden = lax.psum_scatter(
        contract_last(cot_all, weight_out), "row", scatter_dimension=0, tiled=True
    )
    grad_pre = lax.all_gather((grad_hidden * slope).astype(BF), "row", axis=0, tiled=True)
    mixed = lax.psum_scatter(
        jnp.dot(hidden, weight_out, preferred_element_type=F32),
        "col", scatter_dimension=0, tiled=True,
    ).astype(BF)
    grad_tokens = lax.psum_scatter(
        contract_last(grad_pre, weight_in), "col", scatter_dimension=0, tiled=True
    ).astype(BF)
    grad_in = contract_first(tok_all, grad_pre).astype(BF)
    grad_out = contract_first(hidden, cot_all).astype(BF)
    return (mixed, grad_tokens, grad_in, grad_out)


def shards(tokens, cotangent, weight_in, weight_out):
    n, n_col = lax.axis_size("row"), lax.axis_size("col")
    fits = (
        n >= 4
        and n & (n - 1) == 0
        and n_col % CORES == 0
        and tokens.shape[0] % 8 == 0
        and weight_in.shape[0] % 128 == 0
        and weight_in.shape[1] % (128 * n) == 0
        and (tokens.shape[0] * n_col) % 64 == 0
    )
    plan = split_plan if fits else plain_plan
    return plan(tokens, cotangent, weight_in, weight_out)


def solution(mesh):
    return jax.shard_map(
        shards,
        mesh=mesh,
        in_specs=(P("col", "row"), P("col", "row"), P("row", "col"), P("col", "row")),
        out_specs=(P("col", "row"), P("col", "row"), P("row", "col"), P("col", "row")),
        check_vma=False,
    )
```

time: 192 us -> 81.9 us (0.43)
  matrix products: 66.6 us -> 0 us
  blocking collectives: 49.5 us -> 0 us
  Pallas kernels: 0 us -> 48 us
  local copies, waits for them, and re-layouts: 24.6 us -> 0.03 us
  starting transfers between devices: 0.16 us -> 18.3 us
  waiting for transfers between devices: 31.8 us -> 14.6 us
  between operations: 13.8 us -> 0.87 us
  other arithmetic: 4.15 us -> 0.01 us
    dot_general x6 -> x0, matrix products: 66.6 us -> none  [the longest x2 26.2 us: contract_last(): lax.dot_general(left_side, right_side, (((1,), (1,)), ((), ())), preferre...]
    all_gather x4 -> x0, blocking collectives: 49.5 us -> none  [the longest x2 18.7 us: token_spread(): return lax.all_gather(row_piece, 'row', axis=0, tiled=True)]
    pallas_call x0 -> x14, Pallas kernels: none -> 48 us  [call(): pl.pallas_call(kernel, in_specs=[spec for _, spec in args], out_specs=[sp...]
    reduce_scatter x4 -> x0, waiting for transfers between devices: 31.7 us -> none  [the longest x2 31.7 us: width_sums(): lax.psum_scatter(term_fn(jnp.int32(0), lax.axis_size('row') * row_count),...]
    unnamed x3 -> x10, local copies, waits for them, and re-layouts: 24.6 us -> 0.03 us
    ppermute x0 -> x14, starting transfers between devices: none -> 18.3 us  [the longest x6 10.9 us: along(): return lax.ppermute(array, 'col', pairs)]
    ppermute x0 -> x14, waiting for transfers between devices: none -> 14.6 us  [the longest x6 8.33 us: across(): return lax.ppermute(array, 'row', [(i, i ^ step) for i in range(n)])]
    convert_element_type x3 -> x0, other arithmetic: 4.15 us -> none  [the longest x1 1.52 us: shards(): grad_tokens = unit_sums(input_term, col_rows).astype(jnp.bfloat16)]
  transfers between devices with their start and end apart: 4 -> 14, of which waited for: 2 -> 6; matrix products, arithmetic and copies ran while one was open for 36% -> 0% of each run, Pallas kernels for 0% -> 25%
where the time goes in v1:
time: 81.9 us; the launch traced here: 81.7 us
  Pallas kernels  48 us (59%)
  starting transfers between devices  18.3 us (22%)
  waiting for transfers between devices  14.6 us (18%)
  between operations  0.87 us (1%)
    pallas_call x14, Pallas kernels, call(): pl.pallas_call(kernel, in_specs=[spec for _, spec in args], out_specs=[sp...  48 us
    ppermute x6, starting transfers between devices, along(): return lax.ppermute(array, 'col', pairs)  10.9 us
    ppermute x6, waiting for transfers between devices, across(): return lax.ppermute(array, 'row', [(i, i ^ step) for i in range(n)])  8.33 us
    ppermute x6, starting transfers between devices, across(): return lax.ppermute(array, 'row', [(i, i ^ step) for i in range(n)])  7.24 us
    ppermute x2, waiting for transfers between devices, swap(): return lax.ppermute(array, 'col', [(i, i ^ 1) for i in range(n_col)])  3.98 us
    ppermute x6, waiting for transfers between devices, along(): return lax.ppermute(array, 'col', pairs)  2.28 us
  transfers between devices with their start and end apart: 14, of which 6 were waited for; matrix products, arithmetic and copies ran while one was open for 0% of the time, Pallas kernels for 25%

profile of v1, /device:TPU:0, one launch (start us, length us, event | category | flops | bytes accessed | tf_op | source)
XLA Modules:
  0.0 81.7 jit_solution(15082398880597354993)
XLA Ops:
  0.6 0.8 %shard_map.75.after.refs_0_ = bf16[16,3072]{1,0:T(8,128)(2,1)S(1)} custom-call(bf16[8,3072]{1,0:T(8,128)(2,1)} %tok.1, bf16[8,3072]{1,0:T(8,128)(2,1)} %cot.1), custom_call_target="tpu_custom_call" | custom-call | tf_op jit(solution)/shard_map/pallas_call | solution.py:53
  1.5 3.1 %collective-permute-start.2 = (bf16[16,3072]{1,0:T(8,128)(2,1)S(1)}, bf16[16,3072]{1,0:T(8,128)(2,1)S(1)}, u32[]{:S(2)}, u32[]{:S(2)}) collective-permute-start(bf16[16,3072]{1,0:T(8,128)(2,1)S(1)} %shard_map.75.after.refs_0_), channel_id=1, source_target_pairs={{0,2},{2,4},{4,6},{6,0},{1,3},{3,5},{5,7},{7,1},{8,10},{10,12},{12... | collective-permute-start | bytes 294920 | tf_op jit(solution)/shard_map/ppermute | solution.py:322
  4.6 2.6 %collective-permute-start.1 = (bf16[16,3072]{1,0:T(8,128)(2,1)S(1)}, bf16[16,3072]{1,0:T(8,128)(2,1)S(1)}, u32[]{:S(2)}, u32[]{:S(2)}) collective-permute-start(bf16[16,3072]{1,0:T(8,128)(2,1)S(1)} %shard_map.75.after.refs_0_), channel_id=1, source_target_pairs={{0,4},{2,6},{4,0},{6,2},{1,5},{3,7},{5,1},{7,3},{8,12},{10,14},{12... | collective-permute-start | bytes 294920 | tf_op jit(solution)/shard_map/ppermute | solution.py:322
  7.2 1.3 %collective-permute-start = (bf16[16,3072]{1,0:T(8,128)(2,1)S(1)}, bf16[16,3072]{1,0:T(8,128)(2,1)S(1)}, u32[]{:S(2)}, u32[]{:S(2)}) collective-permute-start(bf16[16,3072]{1,0:T(8,128)(2,1)S(1)} %shard_map.75.after.refs_0_), channel_id=1, source_target_pairs={{0,6},{2,0},{4,2},{6,4},{1,7},{3,1},{5,3},{7,5},{8,14},{10,8},{12,... | collective-permute-start | bytes 294920 | tf_op jit(solution)/shard_map/ppermute | solution.py:322
  8.5 6.5 %shard_map.76.after.weight = bf16[3072,3072]{1,0:T(8,128)(2,1)S(1)} custom-call(bf16[16,3072]{1,0:T(8,128)(2,1)S(1)} %shard_map.75.after.refs_0_, bf16[3072,3072]{1,0:T(8,128)(2,1)} %refs_7_.1), custom_call_target="tpu_custom_call" | custom-call | bytes 18874368 | tf_op jit(solution)/shard_map/pallas_call | solution.py:53
  15.1 0.1 collective-permute-start.3
  15.2 1.7 %collective-permute-done.3.other.refs_5_.refs_2_ = bf16[64,3072]{1,0:T(8,128)(2,1)S(1)} collective-permute-done((bf16[64,3072]{1,0:T(8,128)(2,1)S(1)}, bf16[64,3072]{1,0:T(8,128)(2,1)S(1)}, u32[]{:S(2)}, u32[]{:S(2)}) %collective-permute-start.3) | collective-permute-done | bytes 393248 | tf_op jit(solution)/shard_map/ppermute | solution.py:325
  16.9 4.9 %shard_map.78 = (f32[64,768]{1,0:T(8,128)S(1)}, bf16[64,768]{1,0:T(8,128)(2,1)S(1)}, bf16[64,768]{1,0:T(8,128)(2,1)S(1)}, bf16[64,768]{1,0:T(8,128)(2,1)S(1)}) custom-call(bf16[64,3072]{1,0:T(8,128)(2,1)S(1)} %shard_map.77.mine.refs_4_.refs_1_, bf16[64,3072]{1,0:T(8,128)(2,1)S(1)} %collective-permute-done.3.other.refs_5_.refs_2_, ...), custom_call_target="tpu_custom_call" | custom-call | flops 1207959552 | bytes 18874368 | tf_op jit(solution)/shard_map/pallas_call | solution.py:53
  21.8 1.4 %shard_map.82 = bf16[128,768]{1,0:T(8,128)(2,1)S(1)} custom-call(bf16[64,3072]{1,0:T(8,128)(2,1)S(1)} %shard_map.77.mine.refs_4_.refs_1_, bf16[64,3072]{1,0:T(8,128)(2,1)S(1)} %collective-permute-done.3.other.refs_5_.refs_2_, bf16[64,768]{1,0:T(8,128)(2,1)S(1)} %get-tuple-element.26.pre, bf16[3072,3072]{1,0:T(8,128)(2,1)S(1)} %bitcast.1), custom_call_target="tpu_custom_call" | custom-call | flops 301989888 | bytes 4718592 | tf_op jit(solution)/shard_map/pallas_call | solution.py:53
  23.3 1.5 %collective-permute-start.6 = (bf16[128,768]{1,0:T(8,128)(2,1)S(1)}, bf16[128,768]{1,0:T(8,128)(2,1)S(1)}, u32[]{:S(2)}, u32[]{:S(2)}) collective-permute-start(bf16[128,768]{1,0:T(8,128)(2,1)S(1)} %shard_map.82), channel_id=1, source_target_pairs={{0,8},{8,0},{16,24},{24,16},{1,9},{9,1},{17,25},{25,17},{2,10},{10... | collective-permute-start | bytes 589832 | tf_op jit(solution)/shard_map/ppermute | solution.py:328
  24.8 1.4 %shard_map.81 = bf16[128,768]{1,0:T(8,128)(2,1)S(1)} custom-call(bf16[64,3072]{1,0:T(8,128)(2,1)S(1)} %shard_map.77.mine.refs_4_.refs_1_, bf16[64,3072]{1,0:T(8,128)(2,1)S(1)} %collective-permute-done.3.other.refs_5_.refs_2_, bf16[64,768]{1,0:T(8,128)(2,1)S(1)} %get-tuple-element.25.pre, bf16[3072,3072]{1,0:T(8,128)(2,1)S(1)} %bitcast.1), custom_call_target="tpu_custom_call" | custom-call | flops 301989888 | bytes 4718592 | tf_op jit(solution)/shard_map/pallas_call | solution.py:53
  26.2 1.6 %collective-permute-start.5 = (bf16[128,768]{1,0:T(8,128)(2,1)S(1)}, bf16[128,768]{1,0:T(8,128)(2,1)S(1)}, u32[]{:S(2)}, u32[]{:S(2)}) collective-permute-start(bf16[128,768]{1,0:T(8,128)(2,1)S(1)} %shard_map.81), channel_id=1, source_target_pairs={{0,16},{8,24},{16,0},{24,8},{1,17},{9,25},{17,1},{25,9},{2,18},{10... | collective-permute-start | bytes 589832 | tf_op jit(solution)/shard_map/ppermute | solution.py:328
  27.8 1.4 %shard_map.80 = bf16[128,768]{1,0:T(8,128)(2,1)S(1)} custom-call(bf16[64,3072]{1,0:T(8,128)(2,1)S(1)} %shard_map.77.mine.refs_4_.refs_1_, bf16[64,3072]{1,0:T(8,128)(2,1)S(1)} %collective-permute-done.3.other.refs_5_.refs_2_, bf16[64,768]{1,0:T(8,128)(2,1)S(1)} %get-tuple-element.24.pre, bf16[3072,3072]{1,0:T(8,128)(2,1)S(1)} %bitcast.1), custom_call_target="tpu_custom_call" | custom-call | flops 301989888 | bytes 4718592 | tf_op jit(solution)/shard_map/pallas_call | solution.py:53
  29.3 0.5 collective-permute-start.4
  29.8 1.4 %shard_map.79.grad_own = f32[64,768]{1,0:T(8,128)S(1)} custom-call(bf16[64,3072]{1,0:T(8,128)(2,1)S(1)} %shard_map.77.mine.refs_4_.refs_1_, bf16[64,3072]{1,0:T(8,128)(2,1)S(1)} %collective-permute-done.3.other.refs_5_.refs_2_, f32[64,768]{1,0:T(8,128)S(1)} %get-tuple-element.23.pre.pre_own, bf16[3072,3072]{1,0:T(8,128)(2,1)S(1)} %bitcast.1), custom_call_target="tpu_custom_call" | custom-call | flops 301989888 | bytes 4718592 | tf_op jit(solution)/shard_map/pallas_call | solution.py:53
  31.2 5.9 %collective-permute-done.5.refs_1_ = bf16[128,768]{1,0:T(8,128)(2,1)S(1)} collective-permute-done((bf16[128,768]{1,0:T(8,128)(2,1)S(1)}, bf16[128,768]{1,0:T(8,128)(2,1)S(1)}, u32[]{:S(2)}, u32[]{:S(2)}) %collective-permute-start.5) | collective-permute-done | bytes 196640 | tf_op jit(solution)/shard_map/ppermute | solution.py:328
  37.2 0.2 shard_map.83.piece.refs_0_
  37.3 1.6 %collective-permute-start.9 = (bf16[128,768]{1,0:T(8,128)(2,1)S(1)}, bf16[128,768]{1,0:T(8,128)(2,1)S(1)}, u32[]{:S(2)}, u32[]{:S(2)}) collective-permute-start(bf16[128,768]{1,0:T(8,128)(2,1)S(1)} %shard_map.83.piece.refs_0_), channel_id=1, source_target_pairs={{0,24},{8,16},{16,8},{24,0},{1,25},{9,17},{17,9},{25,1},{2,26},{10... | collective-permute-start | bytes 589832 | tf_op jit(solution)/shard_map/ppermute | solution.py:328
  38.9 0.5 collective-permute-start.8
  39.4 1.5 %collective-permute-start.7 = (bf16[128,768]{1,0:T(8,128)(2,1)S(1)}, bf16[128,768]{1,0:T(8,128)(2,1)S(1)}, u32[]{:S(2)}, u32[]{:S(2)}) collective-permute-start(bf16[128,768]{1,0:T(8,128)(2,1)S(1)} %shard_map.83.piece.refs_0_), channel_id=1, source_target_pairs={{0,8},{8,0},{16,24},{24,16},{1,9},{9,1},{17,25},{25,17},{2,10},{10... | collective-permute-start | bytes 589832 | tf_op jit(solution)/shard_map/ppermute | solution.py:328
  40.9 5.1 %shard_map.84 = (bf16[3072,64]{1,0:T(8,128)(2,1)S(1)}, bf16[3072,3072]{1,0:T(8,128)(2,1)}, bf16[3072,3072]{1,0:T(8,128)(2,1)}) custom-call(bf16[128,768]{1,0:T(8,128)(2,1)S(1)} %shard_map.83.piece.refs_0_, bf16[64,3072]{1,0:T(8,128)(2,1)S(1)} %shard_map.77.mine.refs_4_.refs_1_, bf16[64,3072]{1,0:T(8,128)(2,1)S(1)} %collective-permute-done.3.other.refs_5_.refs_2_, ...), custom_call_target="tpu_custom_call" | custom-call | flops 603979776 | bytes 9437184 | tf_op jit(solution)/shard_map/pallas_call | solution.py:53
  46.0 1.5 %collective-permute-done.8.refs_2_ = bf16[128,768]{1,0:T(8,128)(2,1)S(1)} collective-permute-done((bf16[128,768]{1,0:T(8,128)(2,1)S(1)}, bf16[128,768]{1,0:T(8,128)(2,1)S(1)}, u32[]{:S(2)}, u32[]{:S(2)}) %collective-permute-start.8) | collective-permute-done | bytes 196640 | tf_op jit(solution)/shard_map/ppermute | solution.py:328
  47.4 0.9 %collective-permute-done.7.refs_1_ = bf16[128,768]{1,0:T(8,128)(2,1)S(1)} collective-permute-done((bf16[128,768]{1,0:T(8,128)(2,1)S(1)}, bf16[128,768]{1,0:T(8,128)(2,1)S(1)}, u32[]{:S(2)}, u32[]{:S(2)}) %collective-permute-start.7) | collective-permute-done | bytes 196640 | tf_op jit(solution)/shard_map/ppermute | solution.py:328
  48.4 19.3 %shard_map.85 = (f32[64,3072]{1,0:T(8,128)S(1)}, f32[64,3072]{1,0:T(8,128)S(1)}, bf16[3072,3072]{1,0:T(8,128)(2,1)}, bf16[3072,3072]{1,0:T(8,128)(2,1)}) custom-call(bf16[128,768]{1,0:T(8,128)(2,1)S(1)} %shard_map.83.piece.refs_0_, bf16[128,768]{1,0:T(8,128)(2,1)S(1)} %collective-permute-done.7.refs_1_, ...), custom_call_target="tpu_custom_call", output_to_operand_aliasing={{2}: (9, {}), {3}: (10, {})} | custom-call | flops 3623878656 | bytes 56623104 | tf_op jit(solution)/shard_map/pallas_call | solution.py:53
  67.7 2.3 %collective-permute-done.10.away = f32[64,3072]{1,0:T(8,128)S(1)} collective-permute-done((f32[64,3072]{1,0:T(8,128)S(1)}, f32[64,3072]{1,0:T(8,128)S(1)}, u32[]{:S(2)}, u32[]{:S(2)}) %collective-permute-start.10) | collective-permute-done | bytes 786464 | tf_op jit(solution)/shard_map/ppermute | solution.py:325
  70.0 0.1 shard_map.86
  70.1 1.3 %collective-permute-start.11 = (bf16[16,3072]{1,0:T(8,128)(2,1)S(1)}, bf16[16,3072]{1,0:T(8,128)(2,1)S(1)}, u32[]{:S(2)}, u32[]{:S(2)}) collective-permute-start(bf16[16,3072]{1,0:T(8,128)(2,1)S(1)} %get-tuple-element.33), channel_id=1, source_target_pairs={{0,2},{2,4},{4,6},{6,0},{1,3},{3,5},{5,7},{7,1},{8,10},{10,12},{12... | collective-permute-start | bytes 294920 | tf_op jit(solution)/shard_map/ppermute | solution.py:322
  71.3 1.6 %collective-permute-start.12 = (bf16[16,3072]{1,0:T(8,128)(2,1)S(1)}, bf16[16,3072]{1,0:T(8,128)(2,1)S(1)}, u32[]{:S(2)}, u32[]{:S(2)}) collective-permute-start(bf16[16,3072]{1,0:T(8,128)(2,1)S(1)} %get-tuple-element.34), channel_id=1, source_target_pairs={{0,4},{2,6},{4,0},{6,2},{1,5},{3,7},{5,1},{7,3},{8,12},{10,14},{12... | collective-permute-start | bytes 294920 | tf_op jit(solution)/shard_map/ppermute | solution.py:322
  73.0 1.0 %collective-permute-start.13 = (bf16[16,3072]{1,0:T(8,128)(2,1)S(1)}, bf16[16,3072]{1,0:T(8,128)(2,1)S(1)}, u32[]{:S(2)}, u32[]{:S(2)}) collective-permute-start(bf16[16,3072]{1,0:T(8,128)(2,1)S(1)} %get-tuple-element.35), channel_id=1, source_target_pairs={{0,6},{2,0},{4,2},{6,4},{1,7},{3,1},{5,3},{7,5},{8,14},{10,8},{12,... | collective-permute-start | bytes 294920 | tf_op jit(solution)/shard_map/ppermute | solution.py:322
  73.9 4.8 %shard_map.88 = (bf16[3072,3072]{1,0:T(8,128)(2,1)}, bf16[3072,3072]{1,0:T(8,128)(2,1)}) custom-call(bf16[128,768]{1,0:T(8,128)(2,1)S(1)} %collective-permute-done.9.refs_3_.refs_0_, bf16[64,3072]{1,0:T(8,128)(2,1)S(1)} %shard_map.77.mine.refs_4_.refs_1_, ...), custom_call_target="tpu_custom_call", output_to_operand_aliasing={{0}: (4, {}), {1}: (5, {})} | custom-call | flops 603979776 | bytes 9437184 | tf_op jit(solution)/shard_map/pallas_call | solution.py:53
  78.8 2.3 %collective-permute-done.12.refs_2_ = bf16[16,3072]{1,0:T(8,128)(2,1)S(1)} collective-permute-done((bf16[16,3072]{1,0:T(8,128)(2,1)S(1)}, bf16[16,3072]{1,0:T(8,128)(2,1)S(1)}, u32[]{:S(2)}, u32[]{:S(2)}) %collective-permute-start.12) | collective-permute-done | bytes 98336 | tf_op jit(solution)/shard_map/ppermute | solution.py:322
  81.1 0.7 shard_map.87
  (21 shorter events, 0.2 us)
Async XLA Ops:
  1.5 13.6 %collective-permute-start.2 = (bf16[16,3072]{1,0:T(8,128)(2,1)S(1)}, bf16[16,3072]{1,0:T(8,128)(2,1)S(1)}, u32[]{:S(2)}, u32[]{:S(2)}) collective-permute-start(bf16[16,3072]{1,0:T(8,128)(2,1)S(1)} %shard_map.75.after.refs_0_), channel_id=1, source_target_pairs={{0,2},{2,4},{4,6},{6,0},{1,3},{3,5},{5,7},{7,1},{8,10},{10,12},{12... | collective-permute-start | bytes 294920 | tf_op jit(solution)/shard_map/ppermute | solution.py:322
  4.6 10.5 %collective-permute-start.1 = (bf16[16,3072]{1,0:T(8,128)(2,1)S(1)}, bf16[16,3072]{1,0:T(8,128)(2,1)S(1)}, u32[]{:S(2)}, u32[]{:S(2)}) collective-permute-start(bf16[16,3072]{1,0:T(8,128)(2,1)S(1)} %shard_map.75.after.refs_0_), channel_id=1, source_target_pairs={{0,4},{2,6},{4,0},{6,2},{1,5},{3,7},{5,1},{7,3},{8,12},{10,14},{12... | collective-permute-start | bytes 294920 | tf_op jit(solution)/shard_map/ppermute | solution.py:322
  7.2 7.9 %collective-permute-start = (bf16[16,3072]{1,0:T(8,128)(2,1)S(1)}, bf16[16,3072]{1,0:T(8,128)(2,1)S(1)}, u32[]{:S(2)}, u32[]{:S(2)}) collective-permute-start(bf16[16,3072]{1,0:T(8,128)(2,1)S(1)} %shard_map.75.after.refs_0_), channel_id=1, source_target_pairs={{0,6},{2,0},{4,2},{6,4},{1,7},{3,1},{5,3},{7,5},{8,14},{10,8},{12,... | collective-permute-start | bytes 294920 | tf_op jit(solution)/shard_map/ppermute | solution.py:322
  15.0 6.8 %slice-start = ((s8[18874368]{0:T(1024)(128)(4,1)}), s8[4194304]{0:T(1024)(128)(4,1)S(1)}, s32[]{:S(2)}) async-start(s8[18874368]{0:T(1024)(128)(4,1)} %bitcast), calls=%async_computation | async-start | bytes 8388608
  15.0 6.8 %slice-start.1 = ((s8[18874368]{0:T(1024)(128)(4,1)}), s8[4194304]{0:T(1024)(128)(4,1)S(1)}, s32[]{:S(2)}) async-start(s8[18874368]{0:T(1024)(128)(4,1)} %bitcast), calls=%async_computation.1 | async-start | bytes 8388608
  15.0 6.8 %slice-start.2 = ((s8[18874368]{0:T(1024)(128)(4,1)}), s8[4194304]{0:T(1024)(128)(4,1)S(1)}, s32[]{:S(2)}) async-start(s8[18874368]{0:T(1024)(128)(4,1)} %bitcast), calls=%async_computation.2 | async-start | bytes 8388608
  15.1 6.7 %slice-start.3 = ((s8[18874368]{0:T(1024)(128)(4,1)}), s8[4194304]{0:T(1024)(128)(4,1)S(1)}, s32[]{:S(2)}) async-start(s8[18874368]{0:T(1024)(128)(4,1)} %bitcast), calls=%async_computation.3 | async-start | bytes 8388608
  15.1 6.7 %slice-start.4 = ((s8[18874368]{0:T(1024)(128)(4,1)}), s8[2097152]{0:T(1024)(128)(4,1)S(1)}, s32[]{:S(2)}) async-start(s8[18874368]{0:T(1024)(128)(4,1)} %bitcast), calls=%async_computation.4 | async-start | bytes 4194304
  15.1 1.8 %collective-permute-start.3 = (bf16[64,3072]{1,0:T(8,128)(2,1)S(1)}, bf16[64,3072]{1,0:T(8,128)(2,1)S(1)}, u32[]{:S(2)}, u32[]{:S(2)}) collective-permute-start(bf16[64,3072]{1,0:T(8,128)(2,1)S(1)} %shard_map.77.mine.refs_4_.refs_1_), channel_id=1, source_target_pairs={{0,1},{1,0},{2,3},{3,2},{4,5},{5,4},{6,7},{7,6},{8,9},{9,8},{10,11... | collective-permute-start | bytes 1179656 | tf_op jit(solution)/shard_map/ppermute | solution.py:325
  23.3 7.9 %collective-permute-start.6 = (bf16[128,768]{1,0:T(8,128)(2,1)S(1)}, bf16[128,768]{1,0:T(8,128)(2,1)S(1)}, u32[]{:S(2)}, u32[]{:S(2)}) collective-permute-start(bf16[128,768]{1,0:T(8,128)(2,1)S(1)} %shard_map.82), channel_id=1, source_target_pairs={{0,8},{8,0},{16,24},{24,16},{1,9},{9,1},{17,25},{25,17},{2,10},{10... | collective-permute-start | bytes 589832 | tf_op jit(solution)/shard_map/ppermute | solution.py:328
  26.2 10.9 %collective-permute-start.5 = (bf16[128,768]{1,0:T(8,128)(2,1)S(1)}, bf16[128,768]{1,0:T(8,128)(2,1)S(1)}, u32[]{:S(2)}, u32[]{:S(2)}) collective-permute-start(bf16[128,768]{1,0:T(8,128)(2,1)S(1)} %shard_map.81), channel_id=1, source_target_pairs={{0,16},{8,24},{16,0},{24,8},{1,17},{9,25},{17,1},{25,9},{2,18},{10... | collective-permute-start | bytes 589832 | tf_op jit(solution)/shard_map/ppermute | solution.py:328
  29.3 7.9 %collective-permute-start.4 = (bf16[128,768]{1,0:T(8,128)(2,1)S(1)}, bf16[128,768]{1,0:T(8,128)(2,1)S(1)}, u32[]{:S(2)}, u32[]{:S(2)}) collective-permute-start(bf16[128,768]{1,0:T(8,128)(2,1)S(1)} %shard_map.80), channel_id=1, source_target_pairs={{0,24},{8,16},{16,8},{24,0},{1,25},{9,17},{17,9},{25,1},{2,26},{10... | collective-permute-start | bytes 589832 | tf_op jit(solution)/shard_map/ppermute | solution.py:328
  37.3 8.6 %collective-permute-start.9 = (bf16[128,768]{1,0:T(8,128)(2,1)S(1)}, bf16[128,768]{1,0:T(8,128)(2,1)S(1)}, u32[]{:S(2)}, u32[]{:S(2)}) collective-permute-start(bf16[128,768]{1,0:T(8,128)(2,1)S(1)} %shard_map.83.piece.refs_0_), channel_id=1, source_target_pairs={{0,24},{8,16},{16,8},{24,0},{1,25},{9,17},{17,9},{25,1},{2,26},{10... | collective-permute-start | bytes 589832 | tf_op jit(solution)/shard_map/ppermute | solution.py:328
  38.9 8.5 %collective-permute-start.8 = (bf16[128,768]{1,0:T(8,128)(2,1)S(1)}, bf16[128,768]{1,0:T(8,128)(2,1)S(1)}, u32[]{:S(2)}, u32[]{:S(2)}) collective-permute-start(bf16[128,768]{1,0:T(8,128)(2,1)S(1)} %shard_map.83.piece.refs_0_), channel_id=1, source_target_pairs={{0,16},{8,24},{16,0},{24,8},{1,17},{9,25},{17,1},{25,9},{2,18},{10... | collective-permute-start | bytes 589832 | tf_op jit(solution)/shard_map/ppermute | solution.py:328
  39.4 9.0 %collective-permute-start.7 = (bf16[128,768]{1,0:T(8,128)(2,1)S(1)}, bf16[128,768]{1,0:T(8,128)(2,1)S(1)}, u32[]{:S(2)}, u32[]{:S(2)}) collective-permute-start(bf16[128,768]{1,0:T(8,128)(2,1)S(1)} %shard_map.83.piece.refs_0_), channel_id=1, source_target_pairs={{0,8},{8,0},{16,24},{24,16},{1,9},{9,1},{17,25},{25,17},{2,10},{10... | collective-permute-start | bytes 589832 | tf_op jit(solution)/shard_map/ppermute | solution.py:328
  67.6 2.4 %collective-permute-start.10 = (f32[64,3072]{1,0:T(8,128)S(1)}, f32[64,3072]{1,0:T(8,128)S(1)}, u32[]{:S(2)}, u32[]{:S(2)}) collective-permute-start(f32[64,3072]{1,0:T(8,128)S(1)} %get-tuple-element.31), channel_id=1, source_target_pairs={{0,1},{1,0},{2,3},{3,2},{4,5},{5,4},{6,7},{7,6},{8,9},{9,8},{10,11... | collective-permute-start | bytes 2359304 | tf_op jit(solution)/shard_map/ppermute | solution.py:325
  70.1 8.7 %collective-permute-start.11 = (bf16[16,3072]{1,0:T(8,128)(2,1)S(1)}, bf16[16,3072]{1,0:T(8,128)(2,1)S(1)}, u32[]{:S(2)}, u32[]{:S(2)}) collective-permute-start(bf16[16,3072]{1,0:T(8,128)(2,1)S(1)} %get-tuple-element.33), channel_id=1, source_target_pairs={{0,2},{2,4},{4,6},{6,0},{1,3},{3,5},{5,7},{7,1},{8,10},{10,12},{12... | collective-permute-start | bytes 294920 | tf_op jit(solution)/shard_map/ppermute | solution.py:322
  71.3 9.7 %collective-permute-start.12 = (bf16[16,3072]{1,0:T(8,128)(2,1)S(1)}, bf16[16,3072]{1,0:T(8,128)(2,1)S(1)}, u32[]{:S(2)}, u32[]{:S(2)}) collective-permute-start(bf16[16,3072]{1,0:T(8,128)(2,1)S(1)} %get-tuple-element.34), channel_id=1, source_target_pairs={{0,4},{2,6},{4,0},{6,2},{1,5},{3,7},{5,1},{7,3},{8,12},{10,14},{12... | collective-permute-start | bytes 294920 | tf_op jit(solution)/shard_map/ppermute | solution.py:322
  73.0 8.1 %collective-permute-start.13 = (bf16[16,3072]{1,0:T(8,128)(2,1)S(1)}, bf16[16,3072]{1,0:T(8,128)(2,1)S(1)}, u32[]{:S(2)}, u32[]{:S(2)}) collective-permute-start(bf16[16,3072]{1,0:T(8,128)(2,1)S(1)} %get-tuple-element.35), channel_id=1, source_target_pairs={{0,6},{2,0},{4,2},{6,4},{1,7},{3,1},{5,3},{7,5},{8,14},{10,8},{12,... | collective-permute-start | bytes 294920 | tf_op jit(solution)/shard_map/ppermute | solution.py:322
